TPU v7x, 256 devices: a whole 4x4x8 slice. The times are simulated.
256 devices in a mesh: row: 16 (over x_hi, y, core), col: 16 (over z, x_lo).
Axes of the slice: x: 4 (x_hi: 2, x_lo: 2; x = x_hi * 2 + x_lo), y: 4, z: 8, core: 2. Of those that a mesh axis runs over, the one named last changes fastest.
Arguments:
- points: bfloat16 [24576, 768], P('row'), may hold values from -16 to 16
Outputs:
- density: float32 [24576], P(('row', 'col'))
- recon: float32 [24576, 768], P(('row', 'col'))
All inputs are finite; a program needn't handle non-finite values.
Results may differ from a plain program's by a relative error of at most 0.0014.
Values may be sent and summed in bfloat16 or wider, within the bound.
A program may use at most 64 MiB of HBM per device.

v0:
```python
import math

import jax
import jax.numpy as jnp
from jax import lax
from jax.sharding import PartitionSpec as P

NEG = -1e30


def assigned(first_ids, second_ids, span):
    first_stretch = first_ids[:, None] // span
    second_stretch = second_ids[None, :] // span
    parity = (first_stretch + second_stretch) % 2
    same = (first_stretch == second_stretch) & (first_ids[:, None] < second_ids[None, :])
    above = (first_stretch < second_stretch) & (parity == 0)
    below = (first_stretch > second_stretch) & (parity == 1)
    return same | above | below


def combine(row_top, row_sum, row_mix, col_top, col_sum, col_mix):
    top = jnp.maximum(row_top, col_top)
    row_factor = jnp.exp(row_top - top)
    col_factor = jnp.exp(col_top - top)
    total = row_sum * row_factor + col_sum * col_factor
    density = top + jnp.log(total)
    recon = (row_mix * row_factor[:, None] + col_mix * col_factor[:, None]) / total[:, None]
    return (density, recon)


def pair_dot(left, right):
    return lax.dot_general(
        left, right, (((1,), (1,)), ((), ())), preferred_element_type=jnp.float32
    )


def lead_dot(left, right):
    return lax.dot_general(
        left, right, (((0,), (0,)), ((), ())), preferred_element_type=jnp.float32
    )


def maxima(row_local, col_local):
    row_top = lax.pmax(row_local, "col")
    col_top = lax.pmax(col_local, "row")
    return (row_top, col_top)


def shards(points):
    n_row = lax.axis_size("row")
    n_col = lax.axis_size("col")
    block_rows = points.shape[0]
    width = points.shape[1]
    span = block_rows // n_col
    scale = 1.0 / math.sqrt(width)
    row_index = lax.axis_index("row")
    col_index = lax.axis_index("col")
    owned = lax.dynamic_slice_in_dim(points, col_index * span, span, 0)
    neighbours = lax.all_gather(owned, "row", axis=0, tiled=True)
    row_ids = row_index * block_rows + jnp.arange(block_rows, dtype=jnp.int32)
    places = jnp.arange(n_row * span, dtype=jnp.int32)
    col_ids = (places // span * n_col + col_index) * span + places % span
    scores = pair_dot(points, neighbours) * scale
    mask = assigned(row_ids, col_ids, span)
    masked = jnp.where(mask, scores, NEG)
    row_top, col_top = maxima(jnp.max(masked, axis=1), jnp.max(masked, axis=0))
    row_weight = jnp.where(mask, jnp.exp(scores - row_top[:, None]), 0.0).astype(jnp.bfloat16)
    col_weight = jnp.where(mask, jnp.exp(scores - col_top[None, :]), 0.0).astype(jnp.bfloat16)
    row_mix = jnp.dot(row_weight, neighbours, preferred_element_type=jnp.float32)
    row_sum = jnp.sum(row_weight, axis=1, dtype=jnp.float32)
    col_mix = lead_dot(col_weight, points)
    col_sum = jnp.sum(col_weight, axis=0, dtype=jnp.float32)
    own_row_mix, own_row_sum = (
        lax.psum_scatter(row_mix, "col", scatter_dimension=0, tiled=True),
        lax.psum_scatter(row_sum, "col", scatter_dimension=0, tiled=True),
    )
    own_col_mix, own_col_sum = (
        lax.psum_scatter(col_mix, "row", scatter_dimension=0, tiled=True),
        lax.psum_scatter(col_sum, "row", scatter_dimension=0, tiled=True),
    )
    own_row_top = lax.dynamic_slice_in_dim(row_top, col_index * span, span, 0)
    own_col_top = lax.dynamic_slice_in_dim(col_top, row_index * span, span, 0)
    return combine(own_row_top, own_row_sum, own_row_mix, own_col_top, own_col_sum, own_col_mix)


def solution(mesh):
    return jax.shard_map(
        shards,
        mesh=mesh,
        in_specs=(P("row", None),),
        out_specs=(P(("row", "col")), P(("row", "col"), None)),
        check_vma=False,
    )
```

profile of v0, /device:TPU:1, one launch (start us, length us, event | category | flops | bytes accessed | tf_op | source)
XLA Modules:
  0.0 379.3 jit_solution(4510209461478786464)
XLA Ops:
  7.2 0.0 copy-start
  7.2 0.0 all-gather.2.cloned.1.call-start
  7.2 1.6 copy-done
  8.8 0.7 constant_dynamic-slice_fusion
  9.5 0.0 all-gather.2.cloned.1.call-update
  9.5 0.0 reduce-scatter.5.cloned.1.call-start
  9.6 59.4 %all-gather.2.cloned.1.call-done = bf16[1536,768]{1,0:T(8,128)(2,1)} async-done(((bf16[96,768]{1,0:T(8,128)(2,1)}), bf16[1536,768]{1,0:T(8,128)(2,1)}) %all-gather.2.cloned.1.call-update) | async-done | bytes 2359312 | tf_op jit(solution)/shard_map/all_gather | solution.py:59
  69.0 12.3 %fusion.8 = (f32[1536]{0:T(1024)S(1)}, f32[1536,1536]{1,0:T(8,128)}) fusion(s32[1536]{0:T(1024)S(1)} %get-tuple-element.13, s32[1536]{0:T(1024)S(1)} %get-tuple-element.15, s32[1536]{0:T(1024)S(1)} %get-tuple-element.12, s32[1536]{0:T(1024)S(1)} %get-tuple-element.14, bf16[1536,768]{1,0:T(8,128)(2,1)} %all-gather.2.cloned.1.call-done, ...), kind=kOutput, calls=%fused_computation.20 | convolution fusion | flops 3685218816 | bytes 14186496 | tf_op jit(solution)/shard_map/dot_general | solution.py:32
  81.3 27.4 %pmax.14 = f32[1536]{0:T(1024)S(1)} all-reduce(f32[1536]{0:T(1024)S(1)} %get-tuple-element.10), channel_id=1, replica_groups=mesh['row'=16,'col'=16] {'col'}, use_global_device_ids=true, to_apply=%region_1.2 | all-reduce | flops 1536 | bytes 12288 | tf_op jit(solution)/shard_map/pmax | solution.py:44
  108.7 11.1 %convert_reduce_fusion.1 = (f32[1536]{0:T(1024)S(1)}, f32[1536]{0:T(1024)S(1)}) fusion(f32[1536]{0:T(1024)S(1)} %pmax.14, f32[1536,1536]{1,0:T(8,128)} %get-tuple-element.11, s32[1536]{0:T(1024)S(1)} %get-tuple-element.13, s32[1536]{0:T(1024)S(1)} %get-tuple-element.15, s32[1536]{0:T(1024)S(1)} %get-tuple-element.12, s32[1536]{0:T(1024)S(1)} %get-tuple-element.14), kind=kLoop, calls=%fused_computation.17 | loop fusion | flops 70775808 | bytes 9480192 | tf_op jit(solution)/shard_map/reduce_sum | solution.py:70
  119.7 40.3 %pmax.15 = f32[1536]{0:T(1024)S(1)} all-reduce(f32[1536]{0:T(1024)S(1)} %get-tuple-element.3), channel_id=1, replica_groups=mesh['row'=16,'col'=16] {'row'}, use_global_device_ids=true, to_apply=%region_3.4 | all-reduce | flops 1536 | bytes 12288 | tf_op jit(solution)/shard_map/pmax | solution.py:45
  160.0 9.7 %convert_reduce_fusion = (f32[1536]{0:T(1024)S(1)}, bf16[1536,1536]{0,1:T(8,128)(2,1)S(1)}) fusion(f32[1536]{0:T(1024)S(1)} %pmax.15, f32[1536,1536]{1,0:T(8,128)} %get-tuple-element.11, s32[1536]{0:T(1024)S(1)} %get-tuple-element.13, s32[1536]{0:T(1024)S(1)} %get-tuple-element.15, s32[1536]{0:T(1024)S(1)} %get-tuple-element.12, s32[1536]{0:T(1024)S(1)} %get-tuple-element.14), kind=kLoop, calls=%fused_computation.16 | loop fusion | flops 66058752 | bytes 14192640 | tf_op jit(solution)/shard_map/reduce_sum | solution.py:72
  169.7 5.5 %fusion.27 = f32[1536,768]{1,0:T(8,128)} fusion(bf16[1536,1536]{0,1:T(8,128)(2,1)S(1)} %get-tuple-element.9, bf16[1536,768]{1,0:T(8,128)(2,1)S(1)} %copy-done), kind=kOutput, calls=%fused_computation.55 | convolution fusion | flops 3623878656 | bytes 11796480 | tf_op jit(solution)/shard_map/dot_general | solution.py:38
  175.2 0.0 reduce-scatter.5.cloned.1.call-update
  175.3 0.0 copy-start.2
  175.3 0.0 copy-start.1
  175.3 0.2 reduce-scatter.3.cloned.1.call-start
  175.5 16.0 %fusion.23 = f32[1536,768]{1,0:T(8,128)} fusion(bf16[1536,768]{1,0:T(8,128)(2,1)} %all-gather.2.cloned.1.call-done, f32[1536,1536]{1,0:T(8,128)} %get-tuple-element.11, f32[1536]{0:T(1024)S(1)} %pmax.14, s32[1536]{0:T(1024)S(1)} %get-tuple-element.15, s32[1536]{0:T(1024)S(1)} %get-tuple-element.14, s32[1536]{0:T(1024)S(1)} %get-tuple-element.13, ...), kind=kOutput, calls=%fused_computation.54 | convolution fusion | flops 3685220352 | bytes 16545792 | tf_op jit(solution)/shard_map/dot_general | solution.py:69
  191.5 0.0 reduce-scatter.3.cloned.1.call-update
  191.5 0.0 copy-done.2
  191.6 0.6 dynamic-slice
  192.1 0.0 copy-done.1
  192.1 0.6 dynamic-slice.2
  194.0 34.2 %all-reduce.1 = f32[1536]{0:T(1024)S(1)} all-reduce(f32[1536]{0:T(1024)S(1)} %get-tuple-element.8), channel_id=3, replica_groups=mesh['row'=16,'col'=16] {'row'}, use_global_device_ids=true, to_apply=%region_7.8.clone | all-reduce | flops 1536 | bytes 12288
  228.2 24.7 %all-reduce = f32[1536]{0:T(1024)S(1)} all-reduce(f32[1536]{0:T(1024)S(1)} %get-tuple-element.2), channel_id=2, replica_groups=mesh['row'=16,'col'=16] {'col'}, use_global_device_ids=true, to_apply=%region_5.6.clone | all-reduce | flops 1536 | bytes 12288
  252.9 0.6 log_add_fusion
  253.5 6.5 %reduce-scatter.5.cloned.1.call-done = f32[96,768]{1,0:T(8,128)} async-done(((f32[1536,768]{1,0:T(8,128)}), f32[96,768]{1,0:T(8,128)}) %reduce-scatter.5.cloned.1.call-update) | async-done | bytes 294928 | tf_op jit(solution)/shard_map/reduce_scatter | solution.py:78
  260.1 110.8 %reduce-scatter.3.cloned.1.call-done = f32[96,768]{1,0:T(8,128)} async-done(((f32[1536,768]{1,0:T(8,128)}), f32[96,768]{1,0:T(8,128)}) %reduce-scatter.3.cloned.1.call-update) | async-done | bytes 294928 | tf_op jit(solution)/shard_map/reduce_scatter | solution.py:74
  370.9 1.9 add_divide_fusion
  (2 shorter events, 0.0 us)
Async XLA Ops:
  7.2 1.7 copy-start
  7.2 61.8 %all-gather.2.cloned.1.call-start = ((), (), s32[]{:S(2)}) async-start(), calls=%async_computation.2 | async-start | bytes 2506752 | tf_op jit(solution)/shard_map/all_gather | solution.py:59
  9.5 250.5 %reduce-scatter.5.cloned.1.call-start = ((), (), s32[]{:S(2)}) async-start(), calls=%async_computation.4 | async-start | bytes 5013504 | tf_op jit(solution)/shard_map/reduce_scatter | solution.py:78
  175.3 16.3 %copy-start.2 = (u32[256]{0:T(256)S(1)}, u32[256]{0:T(256)}, u32[]{:S(2)}) copy-start(u32[256]{0:T(256)} %constant.68) | copy-start | bytes 3076
  175.3 16.9 %copy-start.1 = (u32[256]{0:T(256)S(1)}, u32[256]{0:T(256)}, u32[]{:S(2)}) copy-start(u32[256]{0:T(256)} %constant.72) | copy-start | bytes 3076
  175.3 195.6 %reduce-scatter.3.cloned.1.call-start = ((), (), s32[]{:S(2)}) async-start(), calls=%async_computation.3 | async-start | bytes 5013504 | tf_op jit(solution)/shard_map/reduce_scatter | solution.py:74
Sparse Core Ops, SparseCore 0:
  11.4 57.6 all-gather.1
  175.4 84.6 reduce-scatter.4
  262.8 108.0 reduce-scatter.2
where the time goes:
time: 381 us; the launch traced here: 379 us
  waiting for transfers between devices  177 us (46%)
  blocking collectives  127 us (33%)
  matrix products  33.8 us (9%)
  other arithmetic  23.3 us (6%)
  between operations  15.2 us (4%)
    reduce_scatter x1, waiting for transfers between devices, shards(): lax.psum_scatter(row_mix, 'col', scatter_dimension=0, tiled=True)  111 us
    all_gather x1, waiting for transfers between devices, shards(): neighbours = lax.all_gather(owned, 'row', axis=0, tiled=True)  59.4 us
    unnamed x2, blocking collectives  58.9 us
    pmax x1, blocking collectives, maxima(): col_top = lax.pmax(col_local, 'row')  40.3 us
    pmax x1, blocking collectives, maxima(): row_top = lax.pmax(row_local, 'col')  27.4 us
    dot_general x1, matrix products, shards(): jnp.dot(row_weight, neighbours, preferred_element_type=jnp.float32)  16 us
    dot_general x1, matrix products, pair_dot(): lax.dot_general(left, right, (((1,), (1,)), ((), ())), preferred_element_...  12.3 us
    reduce_sum x1, other arithmetic, shards(): row_sum = jnp.sum(row_weight, axis=1, dtype=jnp.float32)  11.1 us
  transfers between devices with their start and end apart: 3, of which 3 were waited for; matrix products, arithmetic and copies ran while one was open for 5% of the time, Pallas kernels for 0%

commit v1 on v0

v1 whole, which is shorter than its diff:
```python
import functools
import math

import jax
import jax.numpy as jnp
from jax import lax
from jax.experimental import pallas as pl
from jax.experimental.pallas import tpu as pltpu
from jax.sharding import PartitionSpec as P

MESH = pl.DeviceIdType.MESH
NEG = -1e30
LOG2E = math.log2(math.e)
LN2 = math.log(2.0)

NX, NY, NZ = 4, 4, 8
STEPS = (
    ((0, 0), (1, 0), (-1, 0), (0, 1), (0, -1)),
    ((1, 1), (1, -1), (-1, 1), (-1, -1)),
    ((2, 0), (0, 2)),
    ((1, 2), (-1, 2), (2, 1), (2, -1), (2, 2)),
)
ORDER = (4, 3, -3, 2, -2, 1, -1, 0)
DIRS = {"x+": (1, 0), "x-": (-1, 0), "y+": (0, 1), "y-": (0, -1)}


def wrap(v):
    v %= 4
    return v - 4 if v == 3 else v


def kernel(span, points, recon, density, keys, queries, acc, tops, sums, own_stats,
           in_mix, out_mix, in_last, out_last, in_stats, out_stats,
           load_sem, send_sem, recv_sem, sib_send, sib_recv, mix_send, mix_recv, st_send, st_recv):
    width = points.shape[1]
    half = span // 2
    wide = width // 2
    scale2 = LOG2E / math.sqrt(width)
    row_index, col_index = lax.axis_index("row"), lax.axis_index("col")
    x_hi, y, core = row_index // 8, (row_index // 2) % 4, row_index % 2
    z, x_lo = col_index // 2, col_index % 2
    x = x_hi * 2 + x_lo

    def device(dx=0, dy=0, dz=0, flip=False):
        tx, ty, tz = (x + dx + 4) % 4, (y + dy + 4) % 4, (z + dz + 8) % 8
        tc = 1 - core if flip else core
        return ((tx // 2 * 4 + ty) * 2 + tc, tz * 2 + tx % 2)

    base = {}
    first = []
    total = 0
    for slots in STEPS:
        first.append(total)
        for plane in range(2):
            for slot in slots:
                base[slot, plane] = total
                total += span

    loads = []
    own_rows = pl.ds(pl.multiple_of(col_index * span, span), span)
    own = pltpu.make_async_copy(
        points.at[own_rows], keys.at[pl.ds(base[(0, 0), 0], span)], load_sem.at[0]
    )
    own.start()
    for place, dz in enumerate(ORDER):
        start = pl.multiple_of((((z + dz + 8) % 8) * 2 + x_lo) * span, span)
        load = pltpu.make_async_copy(
            points.at[pl.ds(start, span)], queries.at[pl.ds(place * span, span)], load_sem.at[1 + place]
        )
        load.start()
        loads.append(load)

    barrier = pltpu.get_barrier_semaphore()
    partners = [device(dx=dx, dy=dy) for dx, dy in DIRS.values()]
    partners += [device(dz=1), device(dz=-1), device(flip=True)]
    for partner in partners:
        pl.semaphore_signal(barrier, inc=1, device_id=partner, device_id_type=MESH)
    pl.semaphore_wait(barrier, len(partners))

    messages = {}

    def send(way, slot, part, cols=None):
        dx, dy = DIRS[way]
        target = (wrap(slot[0] - dx), wrap(slot[1] - dy))
        offset = 0 if part == "A" else half
        lanes = pl.ds(0, width) if cols is None else pl.ds(cols * wide, wide)
        number = sum(len(copies) for copies in messages.values())
        copy = pltpu.make_async_remote_copy(
            src_ref=keys.at[pl.ds(base[slot, 0] + offset, half), lanes],
            dst_ref=keys.at[pl.ds(base[target, 0] + offset, half), lanes],
            send_sem=send_sem.at[number],
            recv_sem=recv_sem.at[number],
            device_id=device(dx=dx, dy=dy),
            device_id_type=MESH,
        )
        copy.start()
        messages.setdefault((target, part), []).append(copy)

    def arrived(slot, part):
        for copy in messages[slot, part]:
            copy.wait_recv()

    siblings = {}

    def share(slot):
        number = len(siblings)
        copy = pltpu.make_async_remote_copy(
            src_ref=keys.at[pl.ds(base[slot, 0], span)],
            dst_ref=keys.at[pl.ds(base[slot, 1], span)],
            send_sem=sib_send.at[number],
            recv_sem=sib_recv.at[number],
            device_id=device(flip=True),
            device_id_type=MESH,
        )
        copy.start()
        siblings[slot] = copy

    def attend(step, start, rows, masked_from=None):
        count = 2 * len(STEPS[step]) * span
        mine = pl.ds(start, rows)
        block = keys[pl.ds(first[step], count), :]
        scores = lax.dot_general(
            queries[mine, :], block, (((1,), (1,)), ((), ())), preferred_element_type=jnp.float32
        ) * scale2
        if masked_from is not None:
            r = lax.broadcasted_iota(jnp.int32, scores.shape, 0) - masked_from
            c = lax.broadcasted_iota(jnp.int32, scores.shape, 1)
            scores = jnp.where(r == c, NEG, scores)
        top = jnp.max(scores, axis=1, keepdims=True)
        if step > 0:
            before = tops[mine, 0:1]
            top = jnp.maximum(top, before)
            shrink = jnp.exp2(before - top)
        weight = jnp.exp2(scores - top).astype(jnp.bfloat16)
        mass = jnp.sum(weight.astype(jnp.float32), axis=1, keepdims=True)
        mix = jnp.dot(weight, block, preferred_element_type=jnp.float32)
        if step > 0:
            mass = mass + sums[mine, 0:1] * shrink
            mix = mix + acc[mine, :] * shrink
        acc[mine, :] = mix
        tops[mine, :] = jnp.broadcast_to(top, (rows, 128))
        sums[mine, :] = jnp.broadcast_to(mass, (rows, 128))

    own.wait()
    for way in ("x+", "x-"):
        send(way, (0, 0), "A")
    for way in ("y+", "y-"):
        send(way, (0, 0), "B")
    for way in ("x+", "x-"):
        send(way, (0, 0), "B")
    for way in ("y+", "y-"):
        send(way, (0, 0), "A")
    share((0, 0))
    for load in loads:
        load.wait()

    arrived((-1, 0), "A")
    send("x+", (-1, 0), "A", 0)
    arrived((1, 0), "A")
    send("x-", (1, 0), "A", 1)
    arrived((0, -1), "B")
    send("y+", (0, -1), "B", 0)
    arrived((0, 1), "B")
    send("y-", (0, 1), "B", 1)
    for side in (1, -1):
        for way in ("y+", "y-"):
            send(way, (side, 0), "A")
        for way in ("x+", "x-"):
            send(way, (0, side), "B")
    arrived((-1, 0), "B")
    send("x+", (-1, 0), "B", 0)
    arrived((1, 0), "B")
    send("x-", (1, 0), "B", 1)
    arrived((0, -1), "A")
    send("y+", (0, -1), "A", 0)
    arrived((0, 1), "A")
    send("y-", (0, 1), "A", 1)
    for slot in STEPS[0][1:]:
        share(slot)
    for slot in STEPS[0]:
        siblings[slot].wait_recv()

    group = 2 * span
    last = (len(ORDER) - 1) * span
    attend(0, 0, group)
    attend(0, group, group)
    arrived((2, 0), "A")
    arrived((0, 2), "B")
    for way in ("y+", "y-"):
        send(way, (2, 0), "A")
    for way in ("x+", "x-"):
        send(way, (0, 2), "B")
    attend(0, 2 * group, group)
    attend(0, 3 * group, group, masked_from=span)

    for side in (1, -1):
        arrived((side, -1), "A")
        send("y+", (side, -1), "A", 0)
        arrived((side, 1), "A")
        send("y-", (side, 1), "A", 1)
        arrived((-1, side), "B")
        send("x+", (-1, side), "B", 0)
        arrived((1, side), "B")
        send("x-", (1, side), "B", 1)
    for slot in STEPS[1]:
        share(slot)
    for slot in STEPS[1]:
        siblings[slot].wait_recv()
    attend(1, 0, group)
    attend(1, group, group)

    arrived((2, 0), "B")
    arrived((0, 2), "A")
    for slot in STEPS[2]:
        share(slot)
    arrived((2, -1), "A")
    send("y+", (2, -1), "A", 0)
    arrived((2, 1), "A")
    send("y-", (2, 1), "A", 1)
    arrived((-1, 2), "B")
    send("x+", (-1, 2), "B", 0)
    arrived((1, 2), "B")
    send("x-", (1, 2), "B", 1)
    attend(1, 2 * group, group)
    attend(1, 3 * group, group)
    for slot in STEPS[2]:
        siblings[slot].wait_recv()
    for place in range(4):
        attend(2, place * group, group)
    for side in (1, -1):
        arrived((side, 2), "A")
        share((side, 2))
        arrived((2, side), "B")
        share((2, side))
    arrived((2, 2), "A")
    arrived((2, 2), "B")
    share((2, 2))
    for slot in STEPS[3]:
        siblings[slot].wait_recv()

    def note(place):
        mine = pl.ds(place * span, span)
        lane = lax.broadcasted_iota(jnp.int32, (span, 128), 1)
        pair = jnp.where(lane == 0, tops[mine, :], jnp.where(lane == 1, sums[mine, :], 0.0))
        pair = jnp.concatenate([pair, jnp.zeros((128 - span, 128), jnp.float32)], axis=0)
        own_stats[place] = jnp.transpose(pair)[0:8, :]

    hops = {}

    def start_hop(side, hop, part):
        sign = 1 - 2 * side
        number = (side * 4 + hop) * 2 + part
        if hop < 3:
            source, target = out_mix.at[(side * 3 + hop) * 2 + part], in_mix.at[(side * 3 + hop) * 2 + part]
        else:
            source, target = out_last.at[side * 2 + part], in_last.at[side * 2 + part]
        pair = []
        for src, dst, snd, rcv in (
            (out_stats.at[number], in_stats.at[number], st_send, st_recv),
            (source, target, mix_send, mix_recv),
        ):
            copy = pltpu.make_async_remote_copy(
                src_ref=src, dst_ref=dst, send_sem=snd.at[number], recv_sem=rcv.at[number],
                device_id=device(dz=sign), device_id_type=MESH,
            )
            copy.start()
            pair.append(copy)
        hops[side, hop, part] = pair

    def columns(factors):
        padded = jnp.concatenate([factors, jnp.zeros((128 - factors.shape[0], 128), jnp.float32)], axis=0)
        return jnp.transpose(padded)

    def incoming(side, hop, part):
        for copy in hops[side, hop, part]:
            copy.wait_recv()
        if hop < 3:
            values = in_mix[(side * 3 + hop) * 2 + part].astype(jnp.float32)
        else:
            values = in_last[side * 2 + part]
        stats = in_stats[(side * 4 + hop) * 2 + part]
        return values, stats

    def forward(side, hop, part, merge):
        place = ORDER.index(4 if hop == 0 else (1 - 2 * side) * (4 - hop))
        number = (side * 4 + hop) * 2 + part
        values = acc[pl.ds(place * span + part * half, half), :]
        stats = own_stats[place]
        if merge:
            other, other_stats = incoming(side, hop - 1, part)
            top = jnp.maximum(stats[0:1], other_stats[0:1])
            mine, theirs = jnp.exp2(stats[0:1] - top), jnp.exp2(other_stats[0:1] - top)
            mass = stats[1:2] * mine + other_stats[1:2] * theirs
            out_stats[number, 0:1, :] = top
            out_stats[number, 1:2, :] = mass
            factor = columns(jnp.concatenate([mine, theirs], axis=0))[part * half:(part + 1) * half]
            values = values * factor[:, 0:1] + other * factor[:, 1:2]
        else:
            out_stats[number] = stats
        if hop < 3:
            out_mix[(side * 3 + hop) * 2 + part] = values.astype(jnp.bfloat16)
        else:
            out_last[side * 2 + part] = values
        start_hop(side, hop, part)

    attend(3, 0, span)
    note(0)
    for side in (0, 1):
        forward(side, 0, side, False)
    for hop in (1, 2, 3):
        place = 2 * hop - 1
        attend(3, place * span, group)
        note(place)
        note(place + 1)
        for step in (0, 1):
            for side in (0, 1):
                part = 1 - side if step == 0 else side
                forward(side, hop, part, hop > 1 or part == side)
    attend(3, last, span)
    note(len(ORDER) - 1)

    stats = own_stats[len(ORDER) - 1]
    lane = lax.broadcasted_iota(jnp.int32, (1, 128), 1)
    answer = jnp.zeros((1, 128), jnp.float32)
    for step in (0, 1):
        for part in ((1, 0)[step],):
            plus, plus_stats = incoming(0, 3, part)
            minus, minus_stats = incoming(1, 3, part)
            top = jnp.maximum(stats[0:1], jnp.maximum(plus_stats[0:1], minus_stats[0:1]))
            f0 = jnp.exp2(stats[0:1] - top)
            f1 = jnp.exp2(plus_stats[0:1] - top)
            f2 = jnp.exp2(minus_stats[0:1] - top)
            mass = stats[1:2] * f0 + plus_stats[1:2] * f1 + minus_stats[1:2] * f2
            value = (top + jnp.log2(mass)) * LN2
            answer = jnp.where((lane >= part * half) & (lane < (part + 1) * half), value, answer)
            shares = jnp.concatenate([f0 / mass, f1 / mass, f2 / mass], axis=0)
            factor = columns(shares)[part * half:(part + 1) * half]
            values = acc[pl.ds(last + part * half, half), :] * factor[:, 0:1]
            values = values + plus * factor[:, 1:2] + minus * factor[:, 2:3]
            recon[pl.ds(part * half, half), :] = values
    density[...] = answer[:, :span]

    for copies in messages.values():
        for copy in copies:
            copy.wait_send()
    for copy in siblings.values():
        copy.wait_send()
    for pair in hops.values():
        for copy in pair:
            copy.wait_send()


def shards(points):
    span = points.shape[0] // lax.axis_size("col")
    width = points.shape[1]
    half = span // 2
    dma = pltpu.SemaphoreType.DMA
    vmem = pltpu.VMEM
    recon, density = pl.pallas_call(
        functools.partial(kernel, span),
        out_shape=(
            jax.ShapeDtypeStruct((span, width), jnp.float32),
            jax.ShapeDtypeStruct((1, span), jnp.float32),
        ),
        in_specs=[pl.BlockSpec(memory_space=pl.ANY)],
        out_specs=(pl.BlockSpec(memory_space=pltpu.VMEM), pl.BlockSpec(memory_space=pltpu.VMEM)),
        scratch_shapes=[
            vmem((32 * span, width), jnp.bfloat16),
            vmem((8 * span, width), jnp.bfloat16),
            vmem((8 * span, width), jnp.float32),
            vmem((8 * span, 128), jnp.float32),
            vmem((8 * span, 128), jnp.float32),
            vmem((8, 8, 128), jnp.float32),
            vmem((12, half, width), jnp.bfloat16),
            vmem((12, half, width), jnp.bfloat16),
            vmem((4, half, width), jnp.float32),
            vmem((4, half, width), jnp.float32),
            vmem((16, 8, 128), jnp.float32),
            vmem((16, 8, 128), jnp.float32),
            dma((9,)),
            dma((40,)),
            dma((40,)),
            dma((16,)),
            dma((16,)),
            dma((16,)),
            dma((16,)),
            dma((16,)),
            dma((16,)),
        ],
        compiler_params=pltpu.CompilerParams(
            collective_id=0, has_side_effects=True, vmem_limit_bytes=48 * 1024 * 1024
        ),
        cost_estimate=pl.CostEstimate(
            flops=4 * 8 * span * 32 * span * width,
            bytes_accessed=16 * span * width * 2,
            transcendentals=8 * span * 32 * span,
        ),
    )(points)
    return density.reshape(span), recon


def solution(mesh):
    return jax.shard_map(
        shards,
        mesh=mesh,
        in_specs=(P("row", None),),
        out_specs=(P(("row", "col")), P(("row", "col"), None)),
        check_vma=False,
    )
```

time: 381 us -> 59.9 us (0.16)
  waiting for transfers between devices: 177 us -> 0 us
  blocking collectives: 127 us -> 0 us
  Pallas kernels: 0 us -> 56.3 us
  matrix products: 33.8 us -> 0 us
  other arithmetic: 23.3 us -> 0 us
  between operations: 15.2 us -> 0.65 us
    reduce_scatter x2 -> x0, waiting for transfers between devices: 117 us -> none  [the longest x1 111 us: shards(): lax.psum_scatter(row_mix, 'col', scatter_dimension=0, tiled=True)]
    pmax x2 -> x0, blocking collectives: 67.7 us -> none  [the longest x1 40.3 us: maxima(): col_top = lax.pmax(col_local, 'row')]
    all_gather x1 -> x0, waiting for transfers between devices: 59.4 us -> none  [shards(): neighbours = lax.all_gather(owned, 'row', axis=0, tiled=True)]
    unnamed x2 -> x0, blocking collectives: 58.9 us -> none
    pallas_call x0 -> x1, Pallas kernels: none -> 56.3 us  [shards(): pl.pallas_call(functools.partial(kernel, span), out_shape=(jax.ShapeDtype...]
    dot_general x3 -> x0, matrix products: 33.8 us -> none  [the longest x1 16 us: shards(): jnp.dot(row_weight, neighbours, preferred_element_type=jnp.float32)]
    reduce_sum x2 -> x0, other arithmetic: 20.8 us -> none  [the longest x1 11.1 us: shards(): row_sum = jnp.sum(row_weight, axis=1, dtype=jnp.float32)]
  transfers between devices with their start and end apart: 3 -> 0, of which waited for: 3 -> 0; matrix products, arithmetic and copies ran while one was open for 5% -> 0% of each run, Pallas kernels for 0% -> 0%
where the time goes in v1:
time: 59.9 us; the launch traced here: 59.8 us
  Pallas kernels  56.3 us (94%)
  local copies, waits for them, and re-layouts  2.88 us (5%)
  between operations  0.65 us (1%)
    pallas_call x1, Pallas kernels, shards(): pl.pallas_call(functools.partial(kernel, span), out_shape=(jax.ShapeDtype...  56.3 us
    unnamed x4, local copies, waits for them, and re-layouts  2.88 us

profile of v1, /device:TPU:1, one launch (start us, length us, event | category | flops | bytes accessed | tf_op | source)
XLA Modules:
  0.0 59.8 jit_solution(12968596877884554103)
XLA Ops:
  0.6 0.0 copy-start
  0.6 1.7 %copy-done = bf16[1536,768]{1,0:T(8,128)(2,1)S(1)} copy-done((bf16[1536,768]{1,0:T(8,128)(2,1)S(1)}, bf16[1536,768]{1,0:T(8,128)(2,1)}, u32[]{:S(2)}) %copy-start) | copy-done | bytes 2359320
  2.3 56.3 %shard_map.30 = (f32[96,768]{1,0:T(8,128)S(1)}, f32[1,96]{1,0:T(1,128)S(1)}) custom-call(bf16[1536,768]{1,0:T(8,128)(2,1)S(1)} %copy-done), custom_call_target="tpu_custom_call" | custom-call | flops 7247757312 | bytes 2359296 | tf_op jit(solution)/shard_map/pallas_call | solution.py:359
  58.6 0.5 copy.5
  59.1 0.7 %copy.6 = f32[96,768]{1,0:T(8,128)} copy(f32[96,768]{1,0:T(8,128)S(1)} %get-tuple-element.9) | data formatting | bytes 589824
Async XLA Ops:
  0.6 1.7 %copy-start = (bf16[1536,768]{1,0:T(8,128)(2,1)S(1)}, bf16[1536,768]{1,0:T(8,128)(2,1)}, u32[]{:S(2)}) copy-start(bf16[1536,768]{1,0:T(8,128)(2,1)} %points.1) | copy-start | bytes 7077892

commit v2 on v1

v2 whole, which is shorter than its diff:
```python
import functools
import math

import jax
import jax.numpy as jnp
from jax import lax
from jax.experimental import pallas as pl
from jax.experimental.pallas import tpu as pltpu
from jax.sharding import PartitionSpec as P

MESH = pl.DeviceIdType.MESH
NEG = -1e30
LOG2E = math.log2(math.e)
LN2 = math.log(2.0)

NX, NY, NZ = 4, 4, 8
STEPS = (
    ((0, 0), (1, 0), (-1, 0), (0, 1), (0, -1)),
    ((1, 1), (1, -1), (-1, 1), (-1, -1)),
    ((2, 0), (0, 2)),
    ((1, 2), (-1, 2), (2, 1), (2, -1), (2, 2)),
)
PIECES = 2
SPREAD = 120.0
TINY = 1e-30
ORDER = (4, 3, -3, 2, -2, 1, -1, 0)
DIRS = {"x+": (1, 0), "x-": (-1, 0), "y+": (0, 1), "y-": (0, -1)}


def wrap(v):
    v %= 4
    return v - 4 if v == 3 else v


def kernel(span, points, recon, density, keys, queries, acc, tops, sums, own_stats,
           in_mix, out_mix, in_stats, out_stats,
           load_sem, send_sem, recv_sem, sib_send, sib_recv, mix_send, mix_recv, st_send, st_recv):
    width = points.shape[1]
    half = span // 2
    wide = width // 2
    scale2 = LOG2E / math.sqrt(width)
    row_index, col_index = lax.axis_index("row"), lax.axis_index("col")
    x_hi, y, core = row_index // 8, (row_index // 2) % 4, row_index % 2
    z, x_lo = col_index // 2, col_index % 2
    x = x_hi * 2 + x_lo

    def device(dx=0, dy=0, dz=0, flip=False):
        tx, ty, tz = (x + dx + 4) % 4, (y + dy + 4) % 4, (z + dz + 8) % 8
        tc = 1 - core if flip else core
        return ((tx // 2 * 4 + ty) * 2 + tc, tz * 2 + tx % 2)

    base = {}
    first = []
    total = 0
    for slots in STEPS:
        first.append(total)
        for plane in range(2):
            for slot in slots:
                base[slot, plane] = total
                total += span

    loads = []
    own_rows = pl.ds(pl.multiple_of(col_index * span, span), span)
    own = pltpu.make_async_copy(
        points.at[own_rows], keys.at[pl.ds(base[(0, 0), 0], span)], load_sem.at[0]
    )
    own.start()
    for place, dz in enumerate(ORDER):
        start = pl.multiple_of((((z + dz + 8) % 8) * 2 + x_lo) * span, span)
        load = pltpu.make_async_copy(
            points.at[pl.ds(start, span)], queries.at[pl.ds(place * span, span)], load_sem.at[1 + place]
        )
        load.start()
        loads.append(load)

    barrier = pltpu.get_barrier_semaphore()
    partners = [device(dx=dx, dy=dy) for dx, dy in DIRS.values()]
    partners += [device(dz=1), device(dz=-1), device(flip=True)]
    for partner in partners:
        pl.semaphore_signal(barrier, inc=1, device_id=partner, device_id_type=MESH)
    pl.semaphore_wait(barrier, len(partners))

    messages, seen = {}, set()

    def send(way, slot, part, cols=None):
        dx, dy = DIRS[way]
        target = (wrap(slot[0] - dx), wrap(slot[1] - dy))
        offset = 0 if part == "A" else half
        lanes = pl.ds(0, width) if cols is None else pl.ds(cols * wide, wide)
        number = sum(len(copies) for copies in messages.values())
        copy = pltpu.make_async_remote_copy(
            src_ref=keys.at[pl.ds(base[slot, 0] + offset, half), lanes],
            dst_ref=keys.at[pl.ds(base[target, 0] + offset, half), lanes],
            send_sem=send_sem.at[number],
            recv_sem=recv_sem.at[number],
            device_id=device(dx=dx, dy=dy),
            device_id_type=MESH,
        )
        copy.start()
        messages.setdefault((target, part), []).append(copy)

    def arrived(slot, part):
        if (slot, part) not in seen:
            seen.add((slot, part))
            for copy in messages[slot, part]:
                copy.wait_recv()

    siblings = {}

    def share(slot, part=None):
        number = len(siblings)
        rows = span if part is None else half
        offset = half if part == "B" else 0
        copy = pltpu.make_async_remote_copy(
            src_ref=keys.at[pl.ds(base[slot, 0] + offset, rows)],
            dst_ref=keys.at[pl.ds(base[slot, 1] + offset, rows)],
            send_sem=sib_send.at[number],
            recv_sem=sib_recv.at[number],
            device_id=device(flip=True),
            device_id_type=MESH,
        )
        copy.start()
        siblings[slot, part] = copy

    def attend(step, start, rows, masked_from=None):
        count = 2 * len(STEPS[step]) * span
        mine = pl.ds(start, rows)
        block = keys[pl.ds(first[step], count), :]
        scores = lax.dot_general(
            queries[mine, :], block, (((1,), (1,)), ((), ())), preferred_element_type=jnp.float32
        ) * scale2
        if masked_from is not None:
            r = lax.broadcasted_iota(jnp.int32, scores.shape, 0) - masked_from
            c = lax.broadcasted_iota(jnp.int32, scores.shape, 1)
            scores = jnp.where(r == c, NEG, scores)
        top = jnp.max(scores, axis=1, keepdims=True)
        if step > 0:
            before = tops[mine, 0:1]
            top = jnp.maximum(top, before)
            shrink = jnp.exp2(before - top)
        weight = jnp.exp2(scores - top).astype(jnp.bfloat16)
        mass = jnp.sum(weight.astype(jnp.float32), axis=1, keepdims=True)
        mix = jnp.dot(weight, block, preferred_element_type=jnp.float32)
        if step > 0:
            mass = mass + sums[mine, 0:1] * shrink
            mix = mix + acc[mine, :] * shrink
        acc[mine, :] = mix
        tops[mine, :] = jnp.broadcast_to(top, (rows, 128))
        sums[mine, :] = jnp.broadcast_to(mass, (rows, 128))

    own.wait()
    for way in ("x+", "x-"):
        send(way, (0, 0), "A")
    for way in ("y+", "y-"):
        send(way, (0, 0), "B")
    for way in ("x+", "x-"):
        send(way, (0, 0), "B")
    for way in ("y+", "y-"):
        send(way, (0, 0), "A")
    share((0, 0))
    for load in loads:
        load.wait()

    def pass_on(side_x, part_x, part_y):
        arrived((-1, side_x), part_x)
        send("x+", (-1, side_x), part_x, 0)
        arrived((1, side_x), part_x)
        send("x-", (1, side_x), part_x, 1)
        arrived((side_x, -1), part_y)
        send("y+", (side_x, -1), part_y, 0)
        arrived((side_x, 1), part_y)
        send("y-", (side_x, 1), part_y, 1)

    pass_on(0, "A", "B")
    for side in (1, -1):
        for way in ("y+", "y-"):
            send(way, (side, 0), "A")
        for way in ("x+", "x-"):
            send(way, (0, side), "B")
    for slot in STEPS[0][1:]:
        arrived(slot, "A")
        arrived(slot, "B")
        share(slot)
    arrived((2, 0), "A")
    arrived((0, 2), "B")
    for way in ("y+", "y-"):
        send(way, (2, 0), "A")
    for way in ("x+", "x-"):
        send(way, (0, 2), "B")
    pass_on(0, "B", "A")
    for slot in STEPS[0]:
        siblings[slot, None].wait_recv()

    most = 4 * span
    attend(0, 0, most)
    attend(0, most, most, masked_from=3 * span)

    for side in (1, -1):
        pass_on(side, "B", "A")
    for slot in STEPS[1]:
        share(slot)
    arrived((2, 0), "B")
    arrived((0, 2), "A")
    for slot in STEPS[2]:
        share(slot)
    for slot in STEPS[1]:
        siblings[slot, None].wait_recv()
    attend(1, 0, most)
    pass_on(2, "B", "A")
    for side in (1, -1):
        share((2, side), "A")
        share((side, 2), "B")
    attend(1, most, most)
    for slot in STEPS[2]:
        siblings[slot, None].wait_recv()
    attend(2, 0, most)
    attend(2, most, most)
    for side in (1, -1):
        arrived((side, 2), "A")
        share((side, 2), "A")
        arrived((2, side), "B")
        share((2, side), "B")
    for part in ("A", "B"):
        arrived((2, 2), part)
        share((2, 2), part)
    for slot in STEPS[3]:
        for part in ("A", "B"):
            siblings[slot, part].wait_recv()

    def note(place):
        mine = pl.ds(place * span, span)
        lane = lax.broadcasted_iota(jnp.int32, (span, 128), 1)
        pair = jnp.where(lane == 0, tops[mine, :], jnp.where(lane == 1, sums[mine, :], 0.0))
        pair = jnp.concatenate([pair, jnp.zeros((128 - span, 128), jnp.float32)], axis=0)
        own_stats[place] = jnp.transpose(pair)[0:8, :]

    hops, notes = {}, {}
    piece_width = width // PIECES

    def columns(factors):
        padded = jnp.concatenate([factors, jnp.zeros((128 - factors.shape[0], 128), jnp.float32)], axis=0)
        return jnp.transpose(padded)

    def start_note(side, hop, part):
        number = (side * 4 + hop) * 2 + part
        copy = pltpu.make_async_remote_copy(
            src_ref=out_stats.at[number], dst_ref=in_stats.at[number],
            send_sem=st_send.at[number], recv_sem=st_recv.at[number],
            device_id=device(dz=1 - 2 * side), device_id_type=MESH,
        )
        copy.start()
        notes[side, hop, part] = copy

    def start_piece(side, hop, part, piece):
        number = (side * 4 + hop) * 2 + part
        lanes = pl.ds(piece * piece_width, piece_width)
        copy = pltpu.make_async_remote_copy(
            src_ref=out_mix.at[number, :, lanes], dst_ref=in_mix.at[number, :, lanes],
            send_sem=mix_send.at[number * PIECES + piece], recv_sem=mix_recv.at[number * PIECES + piece],
            device_id=device(dz=1 - 2 * side), device_id_type=MESH,
        )
        copy.start()
        hops[side, hop, part, piece] = copy

    def forward(hop, parts, merge):
        place = [ORDER.index(4 if hop == 0 else (1 - 2 * side) * (4 - hop)) for side in (0, 1)]
        number = [(side * 4 + hop) * 2 + parts[side] for side in (0, 1)]
        factor = [None, None]
        for side in (0, 1):
            stats = own_stats[place[side]]
            if merge:
                notes[side, hop - 1, parts[side]].wait_recv()
                other = in_stats[number[side] - 2]
                top = jnp.maximum(stats[0:1], other[0:1])
                mine, theirs = jnp.exp2(stats[0:1] - top), jnp.exp2(other[0:1] - top)
                out_stats[number[side], 0:1, :] = top
                out_stats[number[side], 1:2, :] = stats[1:2] * mine + other[1:2] * theirs
                first = parts[side] * half
                factor[side] = columns(jnp.concatenate([mine, theirs], axis=0))[first:first + half]
            else:
                out_stats[number[side]] = stats
            if hop < 3:
                start_note(side, hop, parts[side])
        peaks = [jnp.zeros((half, 128), jnp.float32)] * 2
        for piece in range(PIECES):
            lanes = pl.ds(piece * piece_width, piece_width)
            for side in (0, 1):
                values = acc[pl.ds(place[side] * span + parts[side] * half, half), lanes]
                if merge:
                    hops[side, hop - 1, parts[side], piece].wait_recv()
                    other = in_mix[number[side] - 2, :, lanes].astype(jnp.float32)
                    values = values * factor[side][:, 0:1] + other * factor[side][:, 1:2]
                if hop == 3:
                    peak = jnp.maximum(jnp.max(jnp.abs(values), axis=1, keepdims=True), TINY)
                    lane = lax.broadcasted_iota(jnp.int32, (half, 128), 1)
                    peaks[side] = jnp.where(lane == piece, peak, peaks[side])
                    values = jnp.exp2(values * (SPREAD / peak))
                out_mix[number[side], :, lanes] = values.astype(jnp.bfloat16)
                start_piece(side, hop, parts[side], piece)
        if hop == 3:
            for side in (0, 1):
                rows = [peaks[side], jnp.zeros((128 - (parts[side] + 1) * half, 128), jnp.float32)]
                if parts[side]:
                    rows.insert(0, jnp.zeros((parts[side] * half, 128), jnp.float32))
                rows = jnp.transpose(jnp.concatenate(rows, axis=0))
                out_stats[number[side], 2:2 + PIECES, :] = rows[0:PIECES]
                start_note(side, hop, parts[side])

    attend(3, 0, most)
    note(0)
    forward(0, (0, 1), False)
    note(1)
    note(2)
    forward(1, (1, 0), False)
    note(3)
    attend(3, most, most)
    forward(1, (0, 1), True)
    for place in range(4, 8):
        note(place)
    for hop in (2, 3):
        forward(hop, (1, 0), True)
        forward(hop, (0, 1), True)

    last = 7 * span
    stats = own_stats[7]
    lane = lax.broadcasted_iota(jnp.int32, (1, 128), 1)
    answer = jnp.zeros((1, 128), jnp.float32)
    for part in (0, 1):
        for side in (0, 1):
            notes[side, 3, part].wait_recv()
        plus, minus = in_stats[6 + part], in_stats[14 + part]
        top = jnp.maximum(stats[0:1], jnp.maximum(plus[0:1], minus[0:1]))
        f0 = jnp.exp2(stats[0:1] - top)
        f1 = jnp.exp2(plus[0:1] - top)
        f2 = jnp.exp2(minus[0:1] - top)
        mass = stats[1:2] * f0 + plus[1:2] * f1 + minus[1:2] * f2
        value = (top + jnp.log2(mass)) * LN2
        answer = jnp.where((lane >= part * half) & (lane < (part + 1) * half), value, answer)
        shares = [f0 / mass]
        for f, got in ((f1, plus), (f2, minus)):
            shares.append(got[2:2 + PIECES] * (f / (mass * SPREAD)))
        factor = columns(jnp.concatenate(shares, axis=0))[part * half:(part + 1) * half]
        for piece in range(PIECES):
            lanes = pl.ds(piece * piece_width, piece_width)
            values = acc[pl.ds(last + part * half, half), lanes] * factor[:, 0:1]
            for side in (0, 1):
                hops[side, 3, part, piece].wait_recv()
                sent = jnp.log2(in_mix[side * 8 + 6 + part, :, lanes].astype(jnp.float32))
                at = 1 + side * PIECES + piece
                values = values + sent * factor[:, at:at + 1]
            recon[pl.ds(part * half, half), lanes] = values
    density[...] = answer[:, :span]

    for copies in messages.values():
        for copy in copies:
            copy.wait_send()
    for group in (siblings, hops, notes):
        for copy in group.values():
            copy.wait_send()


def shards(points):
    span = points.shape[0] // lax.axis_size("col")
    width = points.shape[1]
    half = span // 2
    dma = pltpu.SemaphoreType.DMA
    vmem = pltpu.VMEM
    recon, density = pl.pallas_call(
        functools.partial(kernel, span),
        out_shape=(
            jax.ShapeDtypeStruct((span, width), jnp.float32),
            jax.ShapeDtypeStruct((1, span), jnp.float32),
        ),
        in_specs=[pl.BlockSpec(memory_space=pltpu.HBM)],
        out_specs=(pl.BlockSpec(memory_space=pltpu.VMEM), pl.BlockSpec(memory_space=pltpu.VMEM)),
        scratch_shapes=[
            vmem((32 * span, width), jnp.bfloat16),
            vmem((8 * span, width), jnp.bfloat16),
            vmem((8 * span, width), jnp.float32),
            vmem((8 * span, 128), jnp.float32),
            vmem((8 * span, 128), jnp.float32),
            vmem((8, 8, 128), jnp.float32),
            vmem((16, half, width), jnp.bfloat16),
            vmem((16, half, width), jnp.bfloat16),
            vmem((16, 8, 128), jnp.float32),
            vmem((16, 8, 128), jnp.float32),
            dma((9,)),
            dma((40,)),
            dma((40,)),
            dma((21,)),
            dma((21,)),
            dma((16 * PIECES,)),
            dma((16 * PIECES,)),
            dma((16,)),
            dma((16,)),
        ],
        compiler_params=pltpu.CompilerParams(
            collective_id=0, has_side_effects=True, vmem_limit_bytes=62 * 1024 * 1024
        ),
        cost_estimate=pl.CostEstimate(
            flops=4 * 8 * span * 32 * span * width,
            bytes_accessed=16 * span * width * 2,
            transcendentals=8 * span * 32 * span,
        ),
    )(points)
    return density.reshape(span), recon


def solution(mesh):
    return jax.shard_map(
        shards,
        mesh=mesh,
        in_specs=(P("row", None),),
        out_specs=(P(("row", "col")), P(("row", "col"), None)),
        check_vma=False,
    )
```

time: 59.9 us -> 53 us (0.88)
  Pallas kernels: 56.3 us -> 49.1 us
    pallas_call x1, Pallas kernels: 56.3 us -> 49.1 us  [shards(): pl.pallas_call(functools.partial(kernel, span), out_shape=(jax.ShapeDtype...]
    unnamed x4 -> x2, local copies, waits for them, and re-layouts: 2.88 us -> 2.88 us
where the time goes in v2:
time: 53 us; the launch traced here: 52.6 us
  Pallas kernels  49.1 us (93%)
  local copies, waits for them, and re-layouts  2.88 us (5%)
  between operations  0.64 us (1%)
    pallas_call x1, Pallas kernels, shards(): pl.pallas_call(functools.partial(kernel, span), out_shape=(jax.ShapeDtype...  49.1 us
    unnamed x2, local copies, waits for them, and re-layouts  2.88 us

profile of v2, /device:TPU:1, one launch (start us, length us, event | category | flops | bytes accessed | tf_op | source)
XLA Modules:
  0.0 52.6 jit_solution(1938018607848564507)
XLA Ops:
  0.6 49.1 %shard_map.30 = (f32[96,768]{1,0:T(8,128)}, f32[1,96]{1,0:T(1,128)}) custom-call(bf16[1536,768]{1,0:T(8,128)(2,1)} %points.1), custom_call_target="tpu_custom_call" | custom-call | flops 7247757312 | bytes 2359296 | tf_op jit(solution)/shard_map/pallas_call | solution.py:368
  49.7 1.2 %copy.5 = f32[96]{0:T(128)} copy(f32[96]{0:T(128)} %bitcast.1) | data formatting | bytes 768
  50.9 1.7 %copy.6 = f32[96,768]{1,0:T(8,128)} copy(f32[96,768]{1,0:T(8,128)} %get-tuple-element.9) | data formatting | bytes 589824

commit v3 on v2

--- a/solution.py
+++ b/solution.py
@@ -32,7 +32,7 @@
     return v - 4 if v == 3 else v
 
 
-def kernel(span, points, recon, density, keys, queries, acc, tops, sums, own_stats,
+def kernel(span, points, recon, density, keys, queries, acc, tops, sums, peaks, own_stats,
            in_mix, out_mix, in_stats, out_stats,
            load_sem, send_sem, recv_sem, sib_send, sib_recv, mix_send, mix_recv, st_send, st_recv):
     width = points.shape[1]
@@ -75,35 +75,40 @@
 
     barrier = pltpu.get_barrier_semaphore()
     partners = [device(dx=dx, dy=dy) for dx, dy in DIRS.values()]
+    partners += [device(dx=dx, dy=dy, flip=True) for dx, dy in DIRS.values()]
     partners += [device(dz=1), device(dz=-1), device(flip=True)]
     for partner in partners:
         pl.semaphore_signal(barrier, inc=1, device_id=partner, device_id_type=MESH)
     pl.semaphore_wait(barrier, len(partners))
 
-    messages, seen = {}, set()
-
-    def send(way, slot, part, cols=None):
+    messages, waited, copies = {}, set(), []
+
+    def send(way, slot, part, cols=None, plane=0):
         dx, dy = DIRS[way]
         target = (wrap(slot[0] - dx), wrap(slot[1] - dy))
         offset = 0 if part == "A" else half
         lanes = pl.ds(0, width) if cols is None else pl.ds(cols * wide, wide)
-        number = sum(len(copies) for copies in messages.values())
         copy = pltpu.make_async_remote_copy(
             src_ref=keys.at[pl.ds(base[slot, 0] + offset, half), lanes],
-            dst_ref=keys.at[pl.ds(base[target, 0] + offset, half), lanes],
-            send_sem=send_sem.at[number],
-            recv_sem=recv_sem.at[number],
-            device_id=device(dx=dx, dy=dy),
+            dst_ref=keys.at[pl.ds(base[target, plane] + offset, half), lanes],
+            send_sem=send_sem.at[len(copies)],
+            recv_sem=recv_sem.at[len(copies)],
+            device_id=device(dx=dx, dy=dy, flip=plane == 1),
             device_id_type=MESH,
         )
         copy.start()
-        messages.setdefault((target, part), []).append(copy)
-
-    def arrived(slot, part):
-        if (slot, part) not in seen:
-            seen.add((slot, part))
-            for copy in messages[slot, part]:
-                copy.wait_recv()
+        messages.setdefault((target, part, plane), []).append((cols, len(copies)))
+        copies.append(copy)
+
+    def send_halves(way, slot, part):
+        for cols in ((0, 1) if way in ("x+", "y+") else (1, 0)):
+            send(way, slot, part, cols)
+
+    def arrived(slot, part, cols=None, plane=0):
+        for held, number in messages[slot, part, plane]:
+            if number not in waited and (cols is None or held is None or held == cols):
+                waited.add(number)
+                copies[number].wait_recv()
 
     siblings = {}
 
@@ -150,9 +155,9 @@
 
     own.wait()
     for way in ("x+", "x-"):
-        send(way, (0, 0), "A")
+        send_halves(way, (0, 0), "A")
     for way in ("y+", "y-"):
-        send(way, (0, 0), "B")
+        send_halves(way, (0, 0), "B")
     for way in ("x+", "x-"):
         send(way, (0, 0), "B")
     for way in ("y+", "y-"):
@@ -161,20 +166,21 @@
     for load in loads:
         load.wait()
 
-    def pass_on(side_x, part_x, part_y):
-        arrived((-1, side_x), part_x)
-        send("x+", (-1, side_x), part_x, 0)
-        arrived((1, side_x), part_x)
-        send("x-", (1, side_x), part_x, 1)
-        arrived((side_x, -1), part_y)
-        send("y+", (side_x, -1), part_y, 0)
-        arrived((side_x, 1), part_y)
-        send("y-", (side_x, 1), part_y, 1)
+    def pass_on(side, part_x, part_y, planes=(0,)):
+        for way, slot, part, cols in (
+            ("x+", (-1, side), part_x, 0), ("x-", (1, side), part_x, 1),
+            ("y+", (side, -1), part_y, 0), ("y-", (side, 1), part_y, 1),
+        ):
+            arrived(slot, part, cols)
+            for plane in planes:
+                send(way, slot, part, cols, plane)
 
     pass_on(0, "A", "B")
     for side in (1, -1):
+        arrived((side, 0), "A")
         for way in ("y+", "y-"):
             send(way, (side, 0), "A")
+        arrived((0, side), "B")
         for way in ("x+", "x-"):
             send(way, (0, side), "B")
     for slot in STEPS[0][1:]:
@@ -182,57 +188,66 @@
         arrived(slot, "B")
         share(slot)
     arrived((2, 0), "A")
+    for way in ("y+", "y-"):
+        send_halves(way, (2, 0), "A")
     arrived((0, 2), "B")
-    for way in ("y+", "y-"):
-        send(way, (2, 0), "A")
     for way in ("x+", "x-"):
-        send(way, (0, 2), "B")
+        send_halves(way, (0, 2), "B")
     pass_on(0, "B", "A")
     for slot in STEPS[0]:
         siblings[slot, None].wait_recv()
 
     most = 4 * span
     attend(0, 0, most)
+    pass_on(1, "B", "A")
     attend(0, most, most, masked_from=3 * span)
-
-    for side in (1, -1):
-        pass_on(side, "B", "A")
+    pass_on(-1, "B", "A")
     for slot in STEPS[1]:
+        arrived(slot, "A")
+        arrived(slot, "B")
         share(slot)
-    arrived((2, 0), "B")
-    arrived((0, 2), "A")
-    for slot in STEPS[2]:
-        share(slot)
+    pass_on(2, "B", "A", (0, 1))
     for slot in STEPS[1]:
         siblings[slot, None].wait_recv()
     attend(1, 0, most)
-    pass_on(2, "B", "A")
+    for slot in STEPS[2]:
+        arrived(slot, "A")
+        arrived(slot, "B")
+        share(slot)
     for side in (1, -1):
+        arrived((2, side), "A")
         share((2, side), "A")
+        arrived((side, 2), "B")
         share((side, 2), "B")
     attend(1, most, most)
     for slot in STEPS[2]:
         siblings[slot, None].wait_recv()
-    attend(2, 0, most)
-    attend(2, most, most)
     for side in (1, -1):
         arrived((side, 2), "A")
         share((side, 2), "A")
         arrived((2, side), "B")
         share((2, side), "B")
+    attend(2, 0, most)
+    attend(2, most, most)
     for part in ("A", "B"):
-        arrived((2, 2), part)
-        share((2, 2), part)
-    for slot in STEPS[3]:
+        for plane in (0, 1):
+            arrived((2, 2), part, plane=plane)
+    for slot in STEPS[3][:4]:
         for part in ("A", "B"):
             siblings[slot, part].wait_recv()
 
-    def note(place):
-        mine = pl.ds(place * span, span)
+    def note(places):
         lane = lax.broadcasted_iota(jnp.int32, (span, 128), 1)
-        pair = jnp.where(lane == 0, tops[mine, :], jnp.where(lane == 1, sums[mine, :], 0.0))
-        pair = jnp.concatenate([pair, jnp.zeros((128 - span, 128), jnp.float32)], axis=0)
-        own_stats[place] = jnp.transpose(pair)[0:8, :]
+        table = jnp.zeros((span, 128), jnp.float32)
+        for index, place in enumerate(places):
+            mine = pl.ds(place * span, span)
+            peak = jnp.maximum(jnp.max(jnp.abs(acc[mine, :]), axis=1, keepdims=True), TINY)
+            peaks[mine, :] = jnp.broadcast_to(peak, (span, 128))
+            for row, values in enumerate((tops[mine, :], sums[mine, :], peak)):
+                table = jnp.where(lane == 3 * index + row, values, table)
+        table = jnp.transpose(jnp.concatenate([table, jnp.zeros((128 - span, 128), jnp.float32)], axis=0))
+        for index, place in enumerate(places):
+            own_stats[place, 0:3, :] = table[3 * index:3 * index + 3]
 
     hops, notes = {}, {}
     piece_width = width // PIECES
@@ -267,56 +282,43 @@
         number = [(side * 4 + hop) * 2 + parts[side] for side in (0, 1)]
         factor = [None, None]
         for side in (0, 1):
+            first = parts[side] * half
             stats = own_stats[place[side]]
             if merge:
                 notes[side, hop - 1, parts[side]].wait_recv()
                 other = in_stats[number[side] - 2]
                 top = jnp.maximum(stats[0:1], other[0:1])
                 mine, theirs = jnp.exp2(stats[0:1] - top), jnp.exp2(other[0:1] - top)
+                peak = stats[2:3] * mine + other[2:3] * theirs
                 out_stats[number[side], 0:1, :] = top
                 out_stats[number[side], 1:2, :] = stats[1:2] * mine + other[1:2] * theirs
-                first = parts[side] * half
-                factor[side] = columns(jnp.concatenate([mine, theirs], axis=0))[first:first + half]
+                out_stats[number[side], 2:3, :] = peak
+                start_note(side, hop, parts[side])
+                shares = [mine * (SPREAD / peak), theirs * (other[2:3] / peak)]
+                factor[side] = columns(jnp.concatenate(shares, axis=0))[first:first + half]
             else:
                 out_stats[number[side]] = stats
-            if hop < 3:
                 start_note(side, hop, parts[side])
-        peaks = [jnp.zeros((half, 128), jnp.float32)] * 2
+                factor[side] = SPREAD / peaks[pl.ds(place[side] * span + first, half), :]
         for piece in range(PIECES):
             lanes = pl.ds(piece * piece_width, piece_width)
             for side in (0, 1):
-                values = acc[pl.ds(place[side] * span + parts[side] * half, half), lanes]
+                values = acc[pl.ds(place[side] * span + parts[side] * half, half), lanes] * factor[side][:, 0:1]
                 if merge:
                     hops[side, hop - 1, parts[side], piece].wait_recv()
-                    other = in_mix[number[side] - 2, :, lanes].astype(jnp.float32)
-                    values = values * factor[side][:, 0:1] + other * factor[side][:, 1:2]
-                if hop == 3:
-                    peak = jnp.maximum(jnp.max(jnp.abs(values), axis=1, keepdims=True), TINY)
-                    lane = lax.broadcasted_iota(jnp.int32, (half, 128), 1)
-                    peaks[side] = jnp.where(lane == piece, peak, peaks[side])
-                    values = jnp.exp2(values * (SPREAD / peak))
-                out_mix[number[side], :, lanes] = values.astype(jnp.bfloat16)
+                    other = jnp.log2(in_mix[number[side] - 2, :, lanes].astype(jnp.float32))
+                    values = values + other * factor[side][:, 1:2]
+                out_mix[number[side], :, lanes] = jnp.exp2(values).astype(jnp.bfloat16)
                 start_piece(side, hop, parts[side], piece)
-        if hop == 3:
-            for side in (0, 1):
-                rows = [peaks[side], jnp.zeros((128 - (parts[side] + 1) * half, 128), jnp.float32)]
-                if parts[side]:
-                    rows.insert(0, jnp.zeros((parts[side] * half, 128), jnp.float32))
-                rows = jnp.transpose(jnp.concatenate(rows, axis=0))
-                out_stats[number[side], 2:2 + PIECES, :] = rows[0:PIECES]
-                start_note(side, hop, parts[side])
-
-    attend(3, 0, most)
-    note(0)
+
+    early = 3 * span
+    attend(3, 0, early)
+    note((0, 1, 2))
     forward(0, (0, 1), False)
-    note(1)
-    note(2)
     forward(1, (1, 0), False)
-    note(3)
-    attend(3, most, most)
+    attend(3, early, 5 * span)
+    note((3, 4, 5, 6, 7))
     forward(1, (0, 1), True)
-    for place in range(4, 8):
-        note(place)
     for hop in (2, 3):
         forward(hop, (1, 0), True)
         forward(hop, (0, 1), True)
@@ -336,9 +338,7 @@
         mass = stats[1:2] * f0 + plus[1:2] * f1 + minus[1:2] * f2
         value = (top + jnp.log2(mass)) * LN2
         answer = jnp.where((lane >= part * half) & (lane < (part + 1) * half), value, answer)
-        shares = [f0 / mass]
-        for f, got in ((f1, plus), (f2, minus)):
-            shares.append(got[2:2 + PIECES] * (f / (mass * SPREAD)))
+        shares = [f0 / mass, f1 * plus[2:3] / (mass * SPREAD), f2 * minus[2:3] / (mass * SPREAD)]
         factor = columns(jnp.concatenate(shares, axis=0))[part * half:(part + 1) * half]
         for piece in range(PIECES):
             lanes = pl.ds(piece * piece_width, piece_width)
@@ -346,14 +346,12 @@
             for side in (0, 1):
                 hops[side, 3, part, piece].wait_recv()
                 sent = jnp.log2(in_mix[side * 8 + 6 + part, :, lanes].astype(jnp.float32))
-                at = 1 + side * PIECES + piece
-                values = values + sent * factor[:, at:at + 1]
+                values = values + sent * factor[:, 1 + side:2 + side]
             recon[pl.ds(part * half, half), lanes] = values
     density[...] = answer[:, :span]
 
-    for copies in messages.values():
-        for copy in copies:
-            copy.wait_send()
+    for copy in copies:
+        copy.wait_send()
     for group in (siblings, hops, notes):
         for copy in group.values():
             copy.wait_send()
@@ -379,16 +377,17 @@
             vmem((8 * span, width), jnp.float32),
             vmem((8 * span, 128), jnp.float32),
             vmem((8 * span, 128), jnp.float32),
+            vmem((8 * span, 128), jnp.float32),
             vmem((8, 8, 128), jnp.float32),
             vmem((16, half, width), jnp.bfloat16),
             vmem((16, half, width), jnp.bfloat16),
             vmem((16, 8, 128), jnp.float32),
             vmem((16, 8, 128), jnp.float32),
             dma((9,)),
-            dma((40,)),
-            dma((40,)),
-            dma((21,)),
-            dma((21,)),
+            dma((52,)),
+            dma((52,)),
+            dma((19,)),
+            dma((19,)),
             dma((16 * PIECES,)),
             dma((16 * PIECES,)),
             dma((16,)),

time: 53 us -> 51.9 us (0.979)
  Pallas kernels: 49.1 us -> 48.1 us
    pallas_call x1, Pallas kernels: 49.1 us -> 48.1 us  [shards(): pl.pallas_call(functools.partial(kernel, span), out_shape=(jax.ShapeDtype...]
where the time goes in v3:
time: 51.9 us; the launch traced here: 51.6 us
  Pallas kernels  48.1 us (93%)
  local copies, waits for them, and re-layouts  2.88 us (6%)
  between operations  0.64 us (1%)
    pallas_call x1, Pallas kernels, shards(): pl.pallas_call(functools.partial(kernel, span), out_shape=(jax.ShapeDtype...  48.1 us
    unnamed x2, local copies, waits for them, and re-layouts  2.88 us

profile of v3, /device:TPU:1, one launch (start us, length us, event | category | flops | bytes accessed | tf_op | source)
XLA Modules:
  0.0 51.6 jit_solution(18210419038619854875)
XLA Ops:
  0.6 48.1 %shard_map.30 = (f32[96,768]{1,0:T(8,128)}, f32[1,96]{1,0:T(1,128)}) custom-call(bf16[1536,768]{1,0:T(8,128)(2,1)} %points.1), custom_call_target="tpu_custom_call" | custom-call | flops 7247757312 | bytes 2359296 | tf_op jit(solution)/shard_map/pallas_call | solution.py:366
  48.7 1.2 %copy.5 = f32[96]{0:T(128)} copy(f32[96]{0:T(128)} %bitcast.1) | data formatting | bytes 768
  49.9 1.7 %copy.6 = f32[96,768]{1,0:T(8,128)} copy(f32[96,768]{1,0:T(8,128)} %get-tuple-element.9) | data formatting | bytes 589824

commit v4 on v3

--- a/solution.py
+++ b/solution.py
@@ -16,8 +16,7 @@
 NX, NY, NZ = 4, 4, 8
 STEPS = (
     ((0, 0), (1, 0), (-1, 0), (0, 1), (0, -1)),
-    ((1, 1), (1, -1), (-1, 1), (-1, -1)),
-    ((2, 0), (0, 2)),
+    ((1, 1), (1, -1), (-1, 1), (-1, -1), (2, 0), (0, 2)),
     ((1, 2), (-1, 2), (2, 1), (2, -1), (2, 2)),
 )
 PIECES = 2
@@ -127,13 +126,17 @@
         copy.start()
         siblings[slot, part] = copy
 
-    def attend(step, start, rows, masked_from=None):
-        count = 2 * len(STEPS[step]) * span
+    def score(step, start, rows):
+        block = keys[pl.ds(first[step], 2 * len(STEPS[step]) * span), :]
+        return lax.dot_general(
+            queries[pl.ds(start, rows), :], block, (((1,), (1,)), ((), ())),
+            preferred_element_type=jnp.float32,
+        )
+
+    def absorb(scores, step, start, rows, masked_from=None):
         mine = pl.ds(start, rows)
-        block = keys[pl.ds(first[step], count), :]
-        scores = lax.dot_general(
-            queries[mine, :], block, (((1,), (1,)), ((), ())), preferred_element_type=jnp.float32
-        ) * scale2
+        block = keys[pl.ds(first[step], 2 * len(STEPS[step]) * span), :]
+        scores = scores * scale2
         if masked_from is not None:
             r = lax.broadcasted_iota(jnp.int32, scores.shape, 0) - masked_from
             c = lax.broadcasted_iota(jnp.int32, scores.shape, 1)
@@ -198,41 +201,35 @@
         siblings[slot, None].wait_recv()
 
     most = 4 * span
-    attend(0, 0, most)
+    near, far = score(0, 0, most), score(0, most, most)
+    absorb(near, 0, 0, most)
     pass_on(1, "B", "A")
-    attend(0, most, most, masked_from=3 * span)
+    absorb(far, 0, most, most, masked_from=3 * span)
     pass_on(-1, "B", "A")
-    for slot in STEPS[1]:
+    for slot in STEPS[1][:4]:
         arrived(slot, "A")
         arrived(slot, "B")
         share(slot)
     pass_on(2, "B", "A", (0, 1))
-    for slot in STEPS[1]:
-        siblings[slot, None].wait_recv()
-    attend(1, 0, most)
-    for slot in STEPS[2]:
+    for slot in STEPS[1][4:]:
         arrived(slot, "A")
         arrived(slot, "B")
         share(slot)
+    for slot in STEPS[1]:
+        siblings[slot, None].wait_recv()
+    near, far = score(1, 0, most), score(1, most, most)
+    absorb(near, 1, 0, most)
     for side in (1, -1):
-        arrived((2, side), "A")
-        share((2, side), "A")
-        arrived((side, 2), "B")
-        share((side, 2), "B")
-    attend(1, most, most)
-    for slot in STEPS[2]:
-        siblings[slot, None].wait_recv()
-    for side in (1, -1):
-        arrived((side, 2), "A")
-        share((side, 2), "A")
-        arrived((2, side), "B")
-        share((2, side), "B")
-    attend(2, 0, most)
-    attend(2, most, most)
+        for part in ("A", "B"):
+            arrived((2, side), part)
+            share((2, side), part)
+            arrived((side, 2), part)
+            share((side, 2), part)
+    absorb(far, 1, most, most)
     for part in ("A", "B"):
         for plane in (0, 1):
             arrived((2, 2), part, plane=plane)
-    for slot in STEPS[3][:4]:
+    for slot in STEPS[2][:4]:
         for part in ("A", "B"):
             siblings[slot, part].wait_recv()
 
@@ -312,11 +309,11 @@
                 start_piece(side, hop, parts[side], piece)
 
     early = 3 * span
-    attend(3, 0, early)
+    absorb(score(2, 0, early), 2, 0, early)
     note((0, 1, 2))
     forward(0, (0, 1), False)
     forward(1, (1, 0), False)
-    attend(3, early, 5 * span)
+    absorb(score(2, early, 5 * span), 2, early, 5 * span)
     note((3, 4, 5, 6, 7))
     forward(1, (0, 1), True)
     for hop in (2, 3):

time: 51.9 us -> 50.6 us (0.975)
  Pallas kernels: 48.1 us -> 46.9 us
    pallas_call x1, Pallas kernels: 48.1 us -> 46.9 us  [shards(): pl.pallas_call(functools.partial(kernel, span), out_shape=(jax.ShapeDtype...]
where the time goes in v4:
time: 50.6 us; the launch traced here: 50.4 us
  Pallas kernels  46.9 us (93%)
  local copies, waits for them, and re-layouts  2.88 us (6%)
  between operations  0.64 us (1%)
    pallas_call x1, Pallas kernels, shards(): pl.pallas_call(functools.partial(kernel, span), out_shape=(jax.ShapeDtype...  46.9 us
    unnamed x2, local copies, waits for them, and re-layouts  2.88 us

profile of v4, /device:TPU:1, one launch (start us, length us, event | category | flops | bytes accessed | tf_op | source)
XLA Modules:
  0.0 50.4 jit_solution(1276826528358221602)
XLA Ops:
  0.6 46.9 %shard_map.30 = (f32[96,768]{1,0:T(8,128)}, f32[1,96]{1,0:T(1,128)}) custom-call(bf16[1536,768]{1,0:T(8,128)(2,1)} %points.1), custom_call_target="tpu_custom_call" | custom-call | flops 7247757312 | bytes 2359296 | tf_op jit(solution)/shard_map/pallas_call | solution.py:363
  47.5 1.2 %copy.5 = f32[96]{0:T(128)} copy(f32[96]{0:T(128)} %bitcast.1) | data formatting | bytes 768
  48.7 1.7 %copy.6 = f32[96,768]{1,0:T(8,128)} copy(f32[96,768]{1,0:T(8,128)} %get-tuple-element.9) | data formatting | bytes 589824

commit v5 on v4

--- a/solution.py
+++ b/solution.py
@@ -202,14 +202,14 @@
 
     most = 4 * span
     near, far = score(0, 0, most), score(0, most, most)
+    pass_on(1, "B", "A")
     absorb(near, 0, 0, most)
-    pass_on(1, "B", "A")
-    absorb(far, 0, most, most, masked_from=3 * span)
     pass_on(-1, "B", "A")
     for slot in STEPS[1][:4]:
         arrived(slot, "A")
         arrived(slot, "B")
         share(slot)
+    absorb(far, 0, most, most, masked_from=3 * span)
     pass_on(2, "B", "A", (0, 1))
     for slot in STEPS[1][4:]:
         arrived(slot, "A")
@@ -218,13 +218,13 @@
     for slot in STEPS[1]:
         siblings[slot, None].wait_recv()
     near, far = score(1, 0, most), score(1, most, most)
-    absorb(near, 1, 0, most)
     for side in (1, -1):
         for part in ("A", "B"):
             arrived((2, side), part)
             share((2, side), part)
             arrived((side, 2), part)
             share((side, 2), part)
+    absorb(near, 1, 0, most)
     absorb(far, 1, most, most)
     for part in ("A", "B"):
         for plane in (0, 1):

time: 50.6 us -> 50.6 us (level)
  no operation moved by 1% of the time
where the time goes in v5:
time: 50.6 us; the launch traced here: 50.5 us
  Pallas kernels  47 us (93%)
  local copies, waits for them, and re-layouts  2.88 us (6%)
  between operations  0.64 us (1%)
    pallas_call x1, Pallas kernels, shards(): pl.pallas_call(functools.partial(kernel, span), out_shape=(jax.ShapeDtype...  47 us
    unnamed x2, local copies, waits for them, and re-layouts  2.88 us

profile of v5, /device:TPU:1, one launch (start us, length us, event | category | flops | bytes accessed | tf_op | source)
XLA Modules:
  0.0 50.5 jit_solution(13825225262026309931)
XLA Ops:
  0.6 47.0 %shard_map.30 = (f32[96,768]{1,0:T(8,128)}, f32[1,96]{1,0:T(1,128)}) custom-call(bf16[1536,768]{1,0:T(8,128)(2,1)} %points.1), custom_call_target="tpu_custom_call" | custom-call | flops 7247757312 | bytes 2359296 | tf_op jit(solution)/shard_map/pallas_call | solution.py:363
  47.6 1.2 %copy.5 = f32[96]{0:T(128)} copy(f32[96]{0:T(128)} %bitcast.1) | data formatting | bytes 768
  48.8 1.7 %copy.6 = f32[96,768]{1,0:T(8,128)} copy(f32[96,768]{1,0:T(8,128)} %get-tuple-element.9) | data formatting | bytes 589824

commit v6 on v5

--- a/solution.py
+++ b/solution.py
@@ -314,8 +314,8 @@
     forward(0, (0, 1), False)
     forward(1, (1, 0), False)
     absorb(score(2, early, 5 * span), 2, early, 5 * span)
+    forward(1, (0, 1), True)
     note((3, 4, 5, 6, 7))
-    forward(1, (0, 1), True)
     for hop in (2, 3):
         forward(hop, (1, 0), True)
         forward(hop, (0, 1), True)
@@ -324,6 +324,7 @@
     stats = own_stats[7]
     lane = lax.broadcasted_iota(jnp.int32, (1, 128), 1)
     answer = jnp.zeros((1, 128), jnp.float32)
+    final = []
     for part in (0, 1):
         for side in (0, 1):
             notes[side, 3, part].wait_recv()
@@ -336,7 +337,8 @@
         value = (top + jnp.log2(mass)) * LN2
         answer = jnp.where((lane >= part * half) & (lane < (part + 1) * half), value, answer)
         shares = [f0 / mass, f1 * plus[2:3] / (mass * SPREAD), f2 * minus[2:3] / (mass * SPREAD)]
-        factor = columns(jnp.concatenate(shares, axis=0))[part * half:(part + 1) * half]
+        final.append(columns(jnp.concatenate(shares, axis=0))[part * half:(part + 1) * half])
+    for part, factor in enumerate(final):
         for piece in range(PIECES):
             lanes = pl.ds(piece * piece_width, piece_width)
             values = acc[pl.ds(last + part * half, half), lanes] * factor[:, 0:1]

time: 50.6 us -> 50.5 us (level)
  no operation moved by 1% of the time
where the time goes in v6:
time: 50.5 us; the launch traced here: 50.4 us
  Pallas kernels  46.8 us (93%)
  local copies, waits for them, and re-layouts  2.88 us (6%)
  between operations  0.64 us (1%)
    pallas_call x1, Pallas kernels, shards(): pl.pallas_call(functools.partial(kernel, span), out_shape=(jax.ShapeDtype...  46.8 us
    unnamed x2, local copies, waits for them, and re-layouts  2.88 us

profile of v6, /device:TPU:1, one launch (start us, length us, event | category | flops | bytes accessed | tf_op | source)
XLA Modules:
  0.0 50.4 jit_solution(10685892505782898367)
XLA Ops:
  0.6 46.8 %shard_map.30 = (f32[96,768]{1,0:T(8,128)}, f32[1,96]{1,0:T(1,128)}) custom-call(bf16[1536,768]{1,0:T(8,128)(2,1)} %points.1), custom_call_target="tpu_custom_call" | custom-call | flops 7247757312 | bytes 2359296 | tf_op jit(solution)/shard_map/pallas_call | solution.py:365
  47.5 1.2 %copy.5 = f32[96]{0:T(128)} copy(f32[96]{0:T(128)} %bitcast.1) | data formatting | bytes 768
  48.7 1.7 %copy.6 = f32[96,768]{1,0:T(8,128)} copy(f32[96,768]{1,0:T(8,128)} %get-tuple-element.9) | data formatting | bytes 589824
